TPU v7x, 256 devices: a whole 4x4x8 slice. The times are simulated.
256 devices in a mesh: mem: 32 (over z, y), cell: 8 (over x, core).
Axes of the slice: x: 4, y: 4, z: 8, core: 2. Of those that a mesh axis runs over, the one named last changes fastest.
Arguments:
- anomaly: bfloat16 [3145728, 256], P(('mem', 'cell')), may hold values from -0.28515625 to 0.28515625
- innovation: float32 [3145728], P(('mem', 'cell')), may hold values from -6 to 6
- obs_weight: float32 [3145728], P(('mem', 'cell')), may hold values from 0.3 to 3
- valid_count: int32 [256], P(('mem', 'cell')), may hold values from 2048 to 12288, as said below
- background: bfloat16 [256, 1048576], P('mem', 'cell'), may hold values from -6 to 6
Outputs:
- analysis: bfloat16 [256, 1048576], P('mem', 'cell')
Inputs may be any that keep to these rules, and one draw needn't show every extreme that they name: The first valid_count[i] of the 12288 row slots of device i hold cloud-free pixels; one device holds exactly 12288.
All inputs are finite; a program needn't handle non-finite values.
Results may differ from a plain program's by a relative error of at most 0.0074.
Values may be sent and summed in bfloat16 or wider, within the bound.
A program may use at most 64 MiB of HBM per device.

v0:
```python
import math

import jax
import jax.numpy as jnp
from jax import lax
from jax.sharding import PartitionSpec as P


def add_blocks(totals, rows_all, misfit_all, first_row, live_rows, block_rows):
    turns = (live_rows + block_rows - 1) // block_rows

    def advance(counter, running):
        offset = first_row + counter * block_rows
        rows_block = lax.dynamic_slice_in_dim(rows_all, offset, block_rows, 0)
        misfit_block = lax.dynamic_slice_in_dim(misfit_all, offset, block_rows, 0)
        gram_part = lax.dot_general(
            rows_block, rows_block, (((0,), (0,)), ((), ())), preferred_element_type=jnp.float32
        )
        pull_part = jnp.dot(misfit_block, rows_block, preferred_element_type=jnp.float32)
        return (running[0] + gram_part, running[1] + pull_part)

    return lax.fori_loop(0, turns, advance, totals)


def send_back(fresh, width):
    members_all = fresh.shape[0]
    return lax.all_to_all(
        fresh.reshape(members_all, 1, width), "mem", split_axis=0, concat_axis=1, tiled=True
    )


def on_device(anomaly, innovation, obs_weight, valid_count, background):
    capacity = anomaly.shape[0]
    members = anomaly.shape[1]
    count_here = valid_count[0]
    live = (jnp.arange(capacity, dtype=jnp.int32) < count_here).astype(jnp.float32)
    row_factor = obs_weight * live
    scaled = (anomaly * row_factor[:, None]).astype(jnp.bfloat16)
    misfit = (innovation * row_factor).astype(jnp.bfloat16)
    totals = (jnp.zeros((members, members), jnp.float32), jnp.zeros((members,), jnp.float32))
    block_rows = math.gcd(capacity, 512)
    gram_local, pull_local = add_blocks(totals, scaled, misfit, 0, count_here, block_rows)
    gram, pull = lax.psum((gram_local, pull_local), ("mem", "cell"))
    precision = gram + (members - 1.0) * jnp.eye(members, dtype=jnp.float32)
    factor = jnp.linalg.cholesky(precision)
    middle = lax.linalg.triangular_solve(factor, pull[:, None], left_side=True, lower=True)
    shift_w = lax.linalg.triangular_solve(
        factor, middle, left_side=True, lower=True, transpose_a=True
    )[:, 0]
    inverse_lower = lax.linalg.triangular_solve(
        factor, jnp.eye(members, dtype=jnp.float32), left_side=True, lower=True
    )
    transform = math.sqrt(members - 1.0) * inverse_lower.T
    weights = (transform + shift_w[:, None]).astype(jnp.bfloat16)
    member_groups = lax.axis_size("mem")
    local_members = background.shape[0]
    arranged = background.reshape(local_members, member_groups, -1)
    block = lax.all_to_all(arranged, "mem", split_axis=1, concat_axis=0, tiled=True)
    width = block.shape[2]
    columns = block.reshape(block.shape[0], width)
    wide = columns.astype(jnp.float32)
    mean_state = jnp.mean(wide, axis=0)
    spread_b = (wide - mean_state).astype(jnp.bfloat16)
    mixed = lax.dot_general(
        weights, spread_b, (((0,), (0,)), ((), ())), preferred_element_type=jnp.float32
    )
    fresh = (mean_state + mixed).astype(jnp.bfloat16)
    result = send_back(fresh, width)
    return result.reshape(local_members, -1)


def solution(mesh):
    in_specs = (
        P(("mem", "cell"), None),
        P(("mem", "cell")),
        P(("mem", "cell")),
        P(("mem", "cell")),
        P("mem", "cell"),
    )
    out_specs = P("mem", "cell")
    return jax.shard_map(
        on_device, mesh=mesh, in_specs=in_specs, out_specs=out_specs, check_vma=False
    )
```

profile of v0, /device:TPU:1, one launch (start us, length us, event | category | flops | bytes accessed | tf_op | source)
XLA Modules:
  0.0 488.5 jit_solution(6762888239601135038)
XLA Ops:
  8.0 7.3 %multiply_convert_fusion = bf16[12288,256]{1,0:T(8,128)(2,1)} fusion(bf16[12288,256]{1,0:T(8,128)(2,1)} %param.7, f32[12288]{0:T(1024)S(1)} %get-tuple-element.100), kind=kLoop, calls=%fused_computation.8 | loop fusion | flops 9437184 | bytes 12632064 | tf_op jit(solution)/shard_map/convert_element_type | solution.py:38
  15.3 25.4 %while.13 = (s32[]{:T(128)}, f32[256,256]{1,0:T(8,128)S(1)}, f32[256]{0:T(256)S(1)}, s32[]{:T(128)}, bf16[12288,256]{1,0:T(8,128)(2,1)}, /*index=5*/bf16[12288]{...) while((s32[]{:T(128)}, f32[256,256]{1,0:T(8,128)S(1)}, f32[256]{0:T(256)S(1)}, s32[]{:T(128)}, ...), condition=%wide.region_2.3_spmd, body=%wide.region_1.2_spmd.sunk | while | flops 67436808 | bytes 1057951 | solution.py:22
  15.5 1.1 fusion.56
  16.6 1.3 convolution_add_fusion.3
  18.0 1.1 fusion.56
  19.1 1.3 convolution_add_fusion.3
  20.5 1.1 fusion.56
  21.6 1.3 convolution_add_fusion.3
  23.1 1.1 fusion.56
  24.2 1.3 convolution_add_fusion.3
  26.7 1.3 convolution_add_fusion.3
  29.3 1.3 convolution_add_fusion.3
  31.8 1.3 convolution_add_fusion.3
  34.3 1.3 convolution_add_fusion.3
  36.9 1.3 convolution_add_fusion.3
  39.4 1.3 convolution_add_fusion.3
  41.6 24.6 %all-to-all-start = ((bf16[8,32,4096]{2,0,1:T(8,128)(2,1)}), bf16[8,32,4096]{2,0,1:T(8,128)(2,1)S(1)}, u32[]{:S(2)}, u32[]{:S(2)}) async-start(bf16[8,32,4096]{2,0,1:T(8,128)(2,1)} %bitcast.100), calls=%async_computation | async-start | bytes 4194304 | tf_op jit(solution)/shard_map/all_to_all | solution.py:58
  66.2 101.9 %psum.15 = f32[256]{0:T(256)S(1)} all-reduce(f32[256]{0:T(256)S(1)} %get-tuple-element.40), channel_id=1, replica_groups=mesh['mem'=32,'cell'=8] {'mem','cell'}, use_global_device_ids=true, to_apply=%region_8.9 | all-reduce | flops 256 | bytes 2048 | tf_op jit(solution)/shard_map/psum | solution.py:43
  168.2 167.2 %all-reduce.3.cloned.1.call-done = f32[256,256]{0,1:T(8,128)} async-done(((f32[256,256]{0,1:T(8,128)}), f32[256,256]{0,1:T(8,128)}) %all-reduce.3.cloned.1.call-update) | async-done | bytes 262160 | tf_op jit(solution)/shard_map/psum | solution.py:43
  337.5 11.7 %cholesky.49 = f32[128,128]{1,0:T(8,128)S(1)} custom-call(f32[128,128]{1,0:T(8,128)S(1)} %cholesky.115), custom_call_target="Cholesky" | custom-call | tf_op jit(solution)/shard_map/jit(cholesky)/cholesky | solution.py:45
  349.4 9.8 %custom-call.18 = f32[1,128,128]{1,2,0:T(8,128)S(1)} custom-call(f32[1,128,128]{2,1,0:T(8,128)S(1)} %get-tuple-element.104), custom_call_target="InvertDiagBlocksLowerTriangular" | custom-call | tf_op jit(solution)/shard_map/jit(cholesky)/cholesky | solution.py:45
  359.8 11.7 %cholesky.103 = f32[128,128]{1,0:T(8,128)S(1)} custom-call(f32[128,128]{1,0:T(8,128)S(1)} %convolution_subtract_fusion.1), custom_call_target="Cholesky" | custom-call | tf_op jit(solution)/shard_map/jit(cholesky)/cholesky | solution.py:45
  373.8 4.3 while.14
  374.4 1.4 dynamic-slice.7
  376.6 1.4 dynamic-slice.7
  378.2 19.9 %custom-call.19 = f32[2,128,128]{1,2,0:T(8,128)S(1)} custom-call(f32[2,128,128]{2,1,0:T(8,128)S(1)} %get-tuple-element.48), custom_call_target="InvertDiagBlocksLowerTriangular" | custom-call | tf_op jit(solution)/shard_map/triangular_solve | solution.py:50
  400.6 2.1 fusion.6
  403.3 3.9 reduce.15
  407.2 3.2 reshape.106
  410.4 58.6 %all_to_all.24 = bf16[32,2,16384]{2,1,0:T(2,128)(2,1)S(1)} all-to-all(bf16[32,2,16384]{2,1,0:T(2,128)(2,1)} %reshape.106), channel_id=1, replica_groups=mesh['mem'=32,'cell'=8] {'mem'}, dimensions={0} | all-to-all | bytes 4194304 | tf_op jit(solution)/shard_map/all_to_all | solution.py:27
  469.0 6.8 %reshape.107 = bf16[256,1,4096]{2,1,0:T(2,128)(2,1)} reshape(bf16[32,2,16384]{2,1,0:T(2,128)(2,1)S(1)} %all_to_all.24) | data formatting | bytes 4194304
  475.8 5.8 %copy.32 = bf16[256,1,4096]{2,0,1:T(8,128)(2,1)} copy(bf16[256,1,4096]{2,1,0:T(2,128)(2,1)} %reshape.107) | data formatting | bytes 4194304
  (84 shorter events, 17.6 us)
Async XLA Ops:
  6.5 328.8 %all-reduce.3.cloned.1.call-start = ((), (), s32[]{:S(2)}) async-start(), calls=%async_computation.2 | async-start | bytes 524288 | tf_op jit(solution)/shard_map/psum | solution.py:43
  41.6 358.6 %all-to-all-start = ((bf16[8,32,4096]{2,0,1:T(8,128)(2,1)}), bf16[8,32,4096]{2,0,1:T(8,128)(2,1)S(1)}, u32[]{:S(2)}, u32[]{:S(2)}) async-start(bf16[8,32,4096]{2,0,1:T(8,128)(2,1)} %bitcast.100), calls=%async_computation | async-start | bytes 4194304 | tf_op jit(solution)/shard_map/all_to_all | solution.py:58
Sparse Core Ops, SparseCore 0:
  41.7 293.6 all-reduce.2
where the time goes:
time: 491 us; the launch traced here: 488 us
  waiting for transfers between devices  167 us (34%)
  blocking collectives  161 us (33%)
  other arithmetic  68.4 us (14%)
  matrix products  28.8 us (6%)
  starting transfers between devices  24.6 us (5%)
  local copies, waits for them, and re-layouts  22.9 us (5%)
  between operations  15.6 us (3%)
    psum x1, waiting for transfers between devices, on_device(): gram, pull = lax.psum((gram_local, pull_local), ('mem', 'cell'))  167 us
    psum x1, blocking collectives, on_device(): gram, pull = lax.psum((gram_local, pull_local), ('mem', 'cell'))  102 us
    all_to_all x1, blocking collectives, send_back(): lax.all_to_all(fresh.reshape(members_all, 1, width), 'mem', split_axis=0,...  58.6 us
    another operation x6, other arithmetic, on_device(): factor = jnp.linalg.cholesky(precision)  34 us
    all_to_all x1, starting transfers between devices, on_device(): lax.all_to_all(arranged, 'mem', split_axis=1, concat_axis=0, tiled=True)  24.6 us
    another operation x3, other arithmetic, on_device(): lax.linalg.triangular_solve(factor, jnp.eye(members, dtype=jnp.float32),...  19.9 us
    unnamed x3, local copies, waits for them, and re-layouts  15.8 us
    dot_general x10, matrix products, advance(): lax.dot_general(rows_block, rows_block, (((0,), (0,)), ((), ())), preferr...  13.1 us
  transfers between devices with their start and end apart: 2, of which 1 were waited for; matrix products, arithmetic and copies ran while one was open for 13% of the time, Pallas kernels for 0%

commit v1 on v0

v1 whole, which is shorter than its diff:
```python
import functools
import math

import jax
import jax.numpy as jnp
from jax import lax
from jax.experimental import pallas as pl
from jax.experimental.pallas import tpu as pltpu
from jax.sharding import PartitionSpec as P

MESH = pl.DeviceIdType.MESH
F32, BF16 = jnp.float32, jnp.bfloat16
EXACT = lax.Precision.HIGHEST
NT = (((1,), (1,)), ((), ()))

Z, Y, X, C = 8, 4, 4, 2
BLOCK, GROUP = 32, 8
CHUNK = 1024
WIDE = 512

TURNS = (
    [(0, 1), (0, 2), (0, 3)] + [(dz, dy) for dy in range(4) for dz in (1, 7)],
    [(2, 0), (6, 0), (2, 1), (6, 1), (2, 2), (6, 2)],
    [(2, 3), (6, 3), (4, 0), (4, 1)],
    [(4, 2), (4, 3), (3, 0), (5, 0)],
    [(3, 1), (5, 1), (3, 2), (5, 2), (3, 3), (5, 3)],
)
MEMBER_PEERS = [offset for turn in TURNS for offset in turn]
PLANE_PEERS = [(dy, dx, dc) for dy in range(Y) for dx in range(X) for dc in range(C)][1:]


def wrapped(base, extent):
    shifted = [base]
    for step in range(1, extent):
        shifted.append(jnp.where(base + step >= extent, base + (step - extent), base + step))
    return shifted


def small_factor(tile, size, group):
    lane = lax.broadcasted_iota(jnp.int32, (size, 128), 1)
    row = lax.broadcasted_iota(jnp.int32, (size, 128), 0)
    work = jnp.where(lane < size, tile, jnp.where(lane - size == row, 1.0, 0.0))

    def tall(piece):
        return jnp.concatenate([piece] * (size // 8), axis=0)

    for first in range(0, size, group):
        spots = range(first, first + group)
        cols = [jnp.broadcast_to(work[:, j : j + 1], (size, 128)) for j in spots]
        rows = [jnp.broadcast_to(work[j : j + 1, :], (8, 128)) for j in spots]
        cross = {
            (u, v): jnp.broadcast_to(cols[v][first + u : first + u + 1, :], (8, 128))
            for v in range(group)
            for u in range(v, group)
        }
        for t in range(group):
            inverse = 1.0 / cross[t, t]
            for u in range(t + 1, group):
                ratio = cross[u, t] * inverse
                rows[u] = rows[u] - ratio * rows[t]
                cols[u] = cols[u] - tall(ratio) * cols[t]
                for v in range(u, group):
                    cross[v, u] = cross[v, u] - ratio * cross[v, t]
            below = jnp.where(row > first + t, cols[t] * tall(inverse), 0.0)
            work = work - below * tall(rows[t])
    diagonal = jnp.sum(jnp.where(lane == row, work, 0.0), axis=1, keepdims=True)
    scale = lax.rsqrt(diagonal)
    scale = scale * (1.5 - 0.5 * diagonal * scale * scale)
    lower = pltpu.roll(work, 128 - size, 1) * scale
    return jnp.where(lane < size, lower, 0.0)


def invert_factor(mat_ref, size, group):
    order = mat_ref.shape[0]
    for first in range(0, order, size):
        last = first + size
        base = first // 128 * 128
        shift = first - base
        rows = mat_ref[first:last, :]
        tile = rows[:, base : base + 128]
        if shift:
            tile = pltpu.roll(tile, 128 - shift, 1)
        inverse = small_factor(tile, size, group)
        panel = jnp.dot(inverse[:, :size], rows, precision=EXACT, preferred_element_type=F32)
        placed = pltpu.roll(inverse, shift, 1) if shift else inverse
        blank = jnp.zeros_like(placed)
        placed = jnp.concatenate([placed if b == base else blank for b in range(0, order, 128)], axis=1)
        lane = lax.broadcasted_iota(jnp.int32, (size, order), 1)
        step = jnp.where((lane >= first) & (lane < last), placed, panel)
        mat_ref[first:last, :] = step
        if last < order:
            left = panel.T[last:, :]
            old = mat_ref[last:, :]
            lane = lax.broadcasted_iota(jnp.int32, old.shape, 1)
            old = jnp.where((lane >= first) & (lane < last), 0.0, old)
            mat_ref[last:, :] = old - jnp.dot(left, step, precision=EXACT, preferred_element_type=F32)


def kernel(
    count_ref, anom_ref, innov_ref, weight_ref, back_ref, out_ref,
    rows_v, innov_v, weight_v, gram_v, parts_v, layers_v, whole_v, mine_v, mat_v, block_v, fresh_v,
    in_sems, fwd_send, fwd_recv, bwd_send, bwd_recv, own_sems,
    plane_send, plane_recv, layer_send, layer_recv, all_send, all_recv,
):
    mem, cell = lax.axis_index("mem"), lax.axis_index("cell")
    z, y = lax.div(mem, Y), lax.rem(mem, Y)
    x, c = lax.div(cell, C), lax.rem(cell, C)
    zs, ys, xs, cs = wrapped(z, Z), wrapped(y, Y), wrapped(x, X), wrapped(c, C)
    capacity, members = rows_v.shape
    groups, local, width = block_v.shape
    chunks = capacity // CHUNK

    def member_dev(offset):
        return (zs[offset[0]] * Y + ys[offset[1]], cell)

    def plane_dev(offset):
        return (z * Y + ys[offset[0]], xs[offset[1]] * C + cs[offset[2]])

    def slot_of(offset):
        return ys[offset[0]] * (X * C) + xs[offset[1]] * C + cs[offset[2]]

    bring = [
        pltpu.make_async_copy(
            anom_ref.at[pl.ds(i * CHUNK, CHUNK), :], rows_v.at[pl.ds(i * CHUNK, CHUNK), :], in_sems.at[i]
        )
        for i in range(chunks)
    ]
    bring.append(pltpu.make_async_copy(innov_ref, innov_v, in_sems.at[chunks]))
    bring.append(pltpu.make_async_copy(weight_ref, weight_v, in_sems.at[chunks + 1]))
    for copy in bring:
        copy.start()

    barrier = pltpu.get_barrier_semaphore()
    for offset in MEMBER_PEERS:
        pl.semaphore_signal(barrier, inc=1, device_id=member_dev(offset), device_id_type=MESH)
    for offset in PLANE_PEERS:
        if offset[1:] != (0, 0):
            pl.semaphore_signal(barrier, inc=1, device_id=plane_dev(offset), device_id_type=MESH)
    pl.semaphore_wait(barrier, len(MEMBER_PEERS) + Y * X * C - Y)

    def block_of(group):
        return pl.ds(pl.multiple_of(group * width, width), width)

    own_in = pltpu.make_async_copy(back_ref.at[:, block_of(mem)], block_v.at[mem], own_sems.at[0])
    own_in.start()
    forward = []

    def send_turn(turn):
        for offset in TURNS[turn]:
            n = len(forward)
            target = member_dev(offset)
            copy = pltpu.make_async_remote_copy(
                src_ref=back_ref.at[:, block_of(target[0])], dst_ref=block_v.at[mem],
                send_sem=fwd_send.at[n], recv_sem=fwd_recv.at[n], device_id=target, device_id_type=MESH,
            )
            copy.start()
            forward.append(copy)

    send_turn(0)

    identity = jnp.where(
        lax.broadcasted_iota(jnp.int32, (members, members), 0)
        == lax.broadcasted_iota(jnp.int32, (members, members), 1),
        1.0, 0.0,
    ).astype(BF16)
    count = count_ref[0]
    bring[chunks].wait()
    bring[chunks + 1].wait()
    gram = jnp.zeros((members, members), F32)
    pull = jnp.zeros((16, members), F32)
    for i in range(chunks):
        bring[i].wait()
        here = pl.ds(i * CHUNK, CHUNK)
        position = i * CHUNK + lax.broadcasted_iota(jnp.int32, (1, CHUNK), 1)
        factor = jnp.where(position < count, weight_v[:, here], 0.0)
        misfit = (innov_v[:, here] * factor).astype(BF16)
        misfit = jnp.broadcast_to(misfit.astype(F32), (16, CHUNK)).astype(BF16)
        flat = lax.dot_general(identity, rows_v[here, :], NT, preferred_element_type=F32)
        scaled = (flat * factor).astype(BF16)
        gram = gram + lax.dot_general(scaled, scaled, NT, preferred_element_type=F32)
        pull = pull + lax.dot_general(misfit, scaled, NT, preferred_element_type=F32)
    row = lax.broadcasted_iota(jnp.int32, (members, members), 0)
    lane = lax.broadcasted_iota(jnp.int32, (members, members), 1)
    pull = pull[:1, :]
    gram = jnp.where((row == 0) & (lane > 0), pull, gram)
    gram = jnp.where((row == 1) & (lane == members - 1), pull[:, :1], gram)
    shards = Y * X * C
    gram_v[...] = gram.reshape(shards, members // shards, members)

    sent = []
    arriving = []
    mine = slot_of((0, 0, 0))
    for n, offset in enumerate(PLANE_PEERS):
        copy = pltpu.make_async_remote_copy(
            src_ref=gram_v.at[slot_of(offset)], dst_ref=parts_v.at[n],
            send_sem=plane_send.at[n], recv_sem=plane_recv.at[n], device_id=plane_dev(offset), device_id_type=MESH,
        )
        copy.start()
        arriving.append(copy)
        sent.append(copy)
    send_turn(1)
    total = gram_v[mine]
    for n, copy in enumerate(arriving):
        copy.wait_recv()
        total = total + parts_v[n]
    mine_v[...] = total
    layers_v[z] = total
    arriving = []
    for step in range(1, Z):
        copy = pltpu.make_async_remote_copy(
            src_ref=mine_v, dst_ref=layers_v.at[z],
            send_sem=layer_send.at[step], recv_sem=layer_recv.at[step],
            device_id=(zs[step] * Y + y, cell), device_id_type=MESH,
        )
        copy.start()
        arriving.append(copy)
        sent.append(copy)
    send_turn(2)
    for copy in arriving:
        copy.wait_recv()
    total = layers_v[0]
    for layer in range(1, Z):
        total = total + layers_v[layer]
    whole_v[mine] = total
    arriving = []
    for n, offset in enumerate(PLANE_PEERS):
        copy = pltpu.make_async_remote_copy(
            src_ref=whole_v.at[mine], dst_ref=whole_v.at[mine],
            send_sem=all_send.at[n], recv_sem=all_recv.at[n], device_id=plane_dev(offset), device_id_type=MESH,
        )
        copy.start()
        arriving.append(copy)
        sent.append(copy)
    send_turn(3)
    for copy in arriving:
        copy.wait_recv()
    send_turn(4)

    packed = whole_v[...].reshape(members, members)
    pull = jnp.where(lane[:1, :] == 0, packed[1:2, members - 1 :], packed[:1, :])
    picks = jnp.where(lax.broadcasted_iota(jnp.int32, (8, members), 1) == 0, 1.0, 0.0)
    column = lax.dot_general(picks, packed, NT, precision=EXACT, preferred_element_type=F32)[:1, :]
    picks = jnp.where(lax.broadcasted_iota(jnp.int32, (8, members), 1) == 1, 1.0, 0.0)
    second = lax.dot_general(picks, packed, NT, precision=EXACT, preferred_element_type=F32)[:1, :]
    precision = jnp.where(row == 0, column, packed)
    precision = jnp.where((row == 1) & (lane == members - 1), second, precision)
    mat_v[...] = precision + jnp.where(row == lane, members - 1.0, 0.0)
    invert_factor(mat_v, BLOCK, GROUP)
    lower = jnp.where(lane <= row, mat_v[...], 0.0)
    middle = lax.dot_general(pull, lower, NT, precision=EXACT, preferred_element_type=F32)
    shift_w = jnp.dot(middle, lower, precision=EXACT, preferred_element_type=F32)
    mixing = (math.sqrt(members - 1.0) * lower + shift_w).astype(BF16)

    own_in.wait()
    for copy in forward:
        copy.wait_recv()
    for copy in forward:
        copy.wait_send()

    for part in range(width // WIDE):
        here = pl.ds(part * WIDE, WIDE)
        values = block_v[:, :, here].astype(F32).reshape(members, WIDE)
        mean = jnp.sum(values, axis=0, keepdims=True) * (1.0 / members)
        spread = (values - mean).astype(BF16)
        fresh = mean + jnp.dot(mixing, spread, preferred_element_type=F32)
        fresh_v[:, :, here] = fresh.reshape(groups, local, WIDE).astype(BF16)

    own_out = pltpu.make_async_copy(fresh_v.at[mem], out_ref.at[:, block_of(mem)], own_sems.at[1])
    own_out.start()
    backward = []
    for n, offset in enumerate(MEMBER_PEERS):
        target = member_dev(offset)
        copy = pltpu.make_async_remote_copy(
            src_ref=fresh_v.at[target[0]], dst_ref=out_ref.at[:, block_of(mem)],
            send_sem=bwd_send.at[n], recv_sem=bwd_recv.at[n], device_id=target, device_id_type=MESH,
        )
        copy.start()
        backward.append(copy)
    own_out.wait()
    for copy in backward:
        copy.wait()
    for copy in sent:
        copy.wait_send()


def on_device(anomaly, innovation, obs_weight, valid_count, background):
    capacity, members = anomaly.shape
    local, cells = background.shape
    groups = lax.axis_size("mem")
    width = cells // groups
    shards = Y * X * C
    share = members // shards
    anywhere = pl.BlockSpec(memory_space=pl.ANY)
    dma = pltpu.SemaphoreType.DMA
    peers = len(MEMBER_PEERS)
    return pl.pallas_call(
        kernel,
        out_shape=jax.ShapeDtypeStruct(background.shape, background.dtype),
        in_specs=[pl.BlockSpec(memory_space=pltpu.SMEM)] + [anywhere] * 4,
        out_specs=anywhere,
        scratch_shapes=[
            pltpu.VMEM((capacity, members), BF16),
            pltpu.VMEM((1, capacity), F32),
            pltpu.VMEM((1, capacity), F32),
            pltpu.VMEM((shards, share, members), F32),
            pltpu.VMEM((shards - 1, share, members), F32),
            pltpu.VMEM((Z, share, members), F32),
            pltpu.VMEM((shards, share, members), F32),
            pltpu.VMEM((share, members), F32),
            pltpu.VMEM((members, members), F32),
            pltpu.VMEM((groups, local, width), BF16),
            pltpu.VMEM((groups, local, width), BF16),
            dma((capacity // CHUNK + 2,)),
            dma((peers,)),
            dma((peers,)),
            dma((peers,)),
            dma((peers,)),
            dma((2,)),
            dma((shards - 1,)),
            dma((shards - 1,)),
            dma((Z,)),
            dma((Z,)),
            dma((shards - 1,)),
            dma((shards - 1,)),
        ],
        compiler_params=pltpu.CompilerParams(
            collective_id=0, has_side_effects=True, vmem_limit_bytes=56 * 2**20
        ),
        name="analysis",
    )(
        valid_count,
        anomaly,
        innovation.reshape(1, capacity),
        obs_weight.reshape(1, capacity),
        background,
    )


def solution(mesh):
    rows = P(("mem", "cell"))
    slab = P("mem", "cell")
    return jax.shard_map(
        on_device,
        mesh=mesh,
        in_specs=(P(("mem", "cell"), None), rows, rows, rows, slab),
        out_specs=slab,
        check_vma=False,
    )
```

time: 491 us -> 126 us (0.26)
  waiting for transfers between devices: 167 us -> 0 us
  blocking collectives: 161 us -> 0 us
  Pallas kernels: 0 us -> 122 us
  other arithmetic: 68.4 us -> 0 us
  matrix products: 28.8 us -> 0 us
  starting transfers between devices: 24.6 us -> 0 us
  local copies, waits for them, and re-layouts: 22.9 us -> 3.05 us
  between operations: 15.6 us -> 0.66 us
    psum x1 -> x0, waiting for transfers between devices: 167 us -> none  [on_device(): gram, pull = lax.psum((gram_local, pull_local), ('mem', 'cell'))]
    pallas_call x0 -> x1, Pallas kernels: none -> 122 us  [on_device(): pl.pallas_call(kernel, out_shape=jax.ShapeDtypeStruct(background.shape, b...]
    psum x1 -> x0, blocking collectives: 102 us -> none  [on_device(): gram, pull = lax.psum((gram_local, pull_local), ('mem', 'cell'))]
    all_to_all x1 -> x0, blocking collectives: 58.6 us -> none  [send_back(): lax.all_to_all(fresh.reshape(members_all, 1, width), 'mem', split_axis=0,...]
    another operation x10 -> x0, other arithmetic: 53.9 us -> none  [the longest x6 34 us: on_device(): factor = jnp.linalg.cholesky(precision)]
    dot_general x21 -> x0, matrix products: 26.1 us -> none  [the longest x10 13.1 us: advance(): lax.dot_general(rows_block, rows_block, (((0,), (0,)), ((), ())), preferr...]
    all_to_all x1 -> x0, starting transfers between devices: 24.6 us -> none  [on_device(): lax.all_to_all(arranged, 'mem', split_axis=1, concat_axis=0, tiled=True)]
    unnamed x3 -> x1, local copies, waits for them, and re-layouts: 15.8 us -> 3.05 us
  transfers between devices with their start and end apart: 2 -> 0, of which waited for: 1 -> 0; matrix products, arithmetic and copies ran while one was open for 13% -> 0% of each run, Pallas kernels for 0% -> 0%
where the time goes in v1:
time: 126 us
  Pallas kernels  122 us (97%)
  local copies, waits for them, and re-layouts  3.05 us (2%)
    pallas_call x1, Pallas kernels, on_device(): pl.pallas_call(kernel, out_shape=jax.ShapeDtypeStruct(background.shape, b...  122 us
    unnamed x1, local copies, waits for them, and re-layouts  3.05 us

profile of v1, /device:TPU:1, one launch (start us, length us, event | category | flops | bytes accessed | tf_op | source)
XLA Modules:
  0.0 125.7 jit_solution(7114743110656000079)
XLA Ops:
  0.7 122.0 %analysis.1 = bf16[8,131072]{1,0:T(8,128)(2,1)} custom-call(s32[1]{0:T(128)S(6)} %copy.7.count_ref, bf16[12288,256]{1,0:T(8,128)(2,1)} %anom_ref.1, f32[1,12288]{1,0:T(1,128)} %bitcast.2, f32[1,12288]{1,0:T(1,128)} %bitcast.3, bf16[8,131072]{1,0:T(8,128)(2,1)} %back_ref.1), custom_call_target="tpu_custom_call" | custom-call | tf_op jit(solution)/shard_map/analysis/pallas_call | solution.py:296
  122.6 3.0 %copy.8 = bf16[8,131072]{1,0:T(8,128)(2,1)} copy(bf16[8,131072]{1,0:T(8,128)(2,1)} %analysis.1) | data formatting | bytes 4194304

commit v2 on v1

v2 whole, which is shorter than its diff:
```python
import itertools
import math

import jax
import jax.numpy as jnp
from jax import lax
from jax.experimental import pallas as pl
from jax.experimental.pallas import tpu as pltpu
from jax.sharding import PartitionSpec as P

MESH = pl.DeviceIdType.MESH
F32, BF16 = jnp.float32, jnp.bfloat16
EXACT = lax.Precision.HIGHEST
NT = (((1,), (1,)), ((), ()))

Z, Y, X, C = 8, 4, 4, 2
BLOCK, GROUP = 64, 8
SPLIT = 2
CHUNK = 2048
WIDE = 512

ORDER = [(dz, dy) for dz in (4, 3, 5, 2, 6, 1, 7, 0) for dy in range(Y) if (dz, dy) != (0, 0)]
FORDER = [(dz, dy) for dys in ((0, 1), (2, 3)) for dz in (1, 7, 2, 6, 0, 4, 3, 5) for dy in dys if (dz, dy) != (0, 0)]
COUNTS = (12, 12, 8, 2, 2, 2, 8)
SCATTER = (("x", "c"), ("y",))
SIZES = {"z": Z, "y": Y, "x": X, "c": C}


def offsets(axes):
    found = []
    for steps in itertools.product(*[range(SIZES[axis]) for axis in axes]):
        if any(steps):
            found.append(dict(zip(axes, steps)))
    return found


def wrapped(base, extent):
    shifted = [base]
    for step in range(1, extent):
        shifted.append(jnp.where(base + step >= extent, base + (step - extent), base + step))
    return shifted


def small_factor(tile, size, group):
    lane = lax.broadcasted_iota(jnp.int32, (size, 128), 1)
    row = lax.broadcasted_iota(jnp.int32, (size, 128), 0)
    work = jnp.where(lane < size, tile, jnp.where(lane - size == row, 1.0, 0.0))

    def tall(piece):
        return jnp.concatenate([piece] * (size // 8), axis=0)

    for first in range(0, size, group):
        spots = range(first, first + group)
        cols = [jnp.broadcast_to(work[:, j : j + 1], (size, 128)) for j in spots]
        rows = [jnp.broadcast_to(work[j : j + 1, :], (8, 128)) for j in spots]
        cross = {
            (u, v): jnp.broadcast_to(cols[v][first + u : first + u + 1, :], (8, 128))
            for v in range(group)
            for u in range(v, group)
        }
        for t in range(group):
            inverse = 1.0 / cross[t, t]
            for u in range(t + 1, group):
                ratio = cross[u, t] * inverse
                rows[u] = rows[u] - ratio * rows[t]
                cols[u] = cols[u] - tall(ratio) * cols[t]
                for v in range(u, group):
                    cross[v, u] = cross[v, u] - ratio * cross[v, t]
            below = jnp.where(row > first + t, cols[t] * tall(inverse), 0.0)
            work = work - below * tall(rows[t])
    diagonal = jnp.sum(jnp.where(lane == row, work, 0.0), axis=1, keepdims=True)
    scale = lax.rsqrt(diagonal)
    scale = scale * (1.5 - 0.5 * diagonal * scale * scale)
    lower = pltpu.roll(work, 128 - size, 1) * scale
    return jnp.where(lane < size, lower, 0.0)


def invert_factor(mat_ref, size, group):
    order = mat_ref.shape[0]
    for first in range(0, order, size):
        last = first + size
        base = first // 128 * 128
        shift = first - base
        rows = mat_ref[first:last, :]
        tile = rows[:, base : base + 128]
        if shift:
            tile = pltpu.roll(tile, 128 - shift, 1)
        inverse = small_factor(tile, size, group)
        panel = jnp.dot(inverse[:, :size], rows, precision=EXACT, preferred_element_type=F32)
        placed = pltpu.roll(inverse, shift, 1) if shift else inverse
        blank = jnp.zeros_like(placed)
        placed = jnp.concatenate([placed if b == base else blank for b in range(0, order, 128)], axis=1)
        lane = lax.broadcasted_iota(jnp.int32, (size, order), 1)
        step = jnp.where((lane >= first) & (lane < last), placed, panel)
        mat_ref[first:last, :] = step
        if last < order:
            left = panel.T[last:, :]
            old = mat_ref[last:, :]
            lane = lax.broadcasted_iota(jnp.int32, old.shape, 1)
            old = jnp.where((lane >= first) & (lane < last), 0.0, old)
            mat_ref[last:, :] = old - jnp.dot(left, step, precision=EXACT, preferred_element_type=F32)


def kernel(
    count_ref, anom_ref, innov_ref, weight_ref, back_ref, out_ref,
    rows_v, scaled_v, misfit_v, innov_v, weight_v, gram_v, layers_v, mat_v, block_v, fresh_v,
    in_sems, fwd_send, fwd_recv, bwd_send, bwd_recv, own_sems, sum_send, sum_recv, *steps_v,
):
    mem, cell = lax.axis_index("mem"), lax.axis_index("cell")
    place = {
        "z": wrapped(lax.div(mem, Y), Z),
        "y": wrapped(lax.rem(mem, Y), Y),
        "x": wrapped(lax.div(cell, C), X),
        "c": wrapped(lax.rem(cell, C), C),
    }
    capacity, members = rows_v.shape
    groups, local, width = block_v.shape
    chunks = capacity // CHUNK
    z = place["z"][0]

    def device(offset):
        at = {axis: place[axis][offset.get(axis, 0)] for axis in "zyxc"}
        return (at["z"] * Y + at["y"], at["x"] * C + at["c"])

    def index(axes, offset):
        at = 0
        for axis in axes:
            at = at * SIZES[axis] + place[axis][offset.get(axis, 0)]
        return at

    def member_dev(offset):
        return device({"z": offset[0], "y": offset[1]})

    bring = [
        pltpu.make_async_copy(
            anom_ref.at[pl.ds(i * CHUNK, CHUNK), :], rows_v.at[pl.ds(i * CHUNK, CHUNK), :], in_sems.at[i]
        )
        for i in range(chunks)
    ]
    bring.append(pltpu.make_async_copy(innov_ref, innov_v, in_sems.at[chunks]))
    bring.append(pltpu.make_async_copy(weight_ref, weight_v, in_sems.at[chunks + 1]))
    for copy in bring:
        copy.start()

    barrier = pltpu.get_barrier_semaphore()
    greeted = [{"z": dz, "y": dy} for dz, dy in ORDER]
    for axes in SCATTER:
        for offset in offsets(axes):
            if not set(axes) <= {"z", "y"}:
                if any(offset.get(axis, 0) for axis in "xc"):
                    greeted.append(offset)
    for offset in greeted:
        pl.semaphore_signal(barrier, inc=1, device_id=device(offset), device_id_type=MESH)
    pl.semaphore_wait(barrier, len(greeted))

    narrow = width // SPLIT

    def cells_of(group, part):
        return pl.ds(pl.multiple_of(group * width + part * narrow, narrow), narrow)

    own_in = pltpu.make_async_copy(
        back_ref.at[:, pl.ds(pl.multiple_of(mem * width, width), width)], block_v.at[mem], own_sems.at[0]
    )
    own_in.start()
    waiting = [(part, offset) for part in range(SPLIT) for offset in FORDER]
    forward = []

    def pump(count):
        for part, offset in waiting[len(forward) : len(forward) + count]:
            n = len(forward)
            target = member_dev(offset)
            copy = pltpu.make_async_remote_copy(
                src_ref=back_ref.at[:, cells_of(target[0], part)],
                dst_ref=block_v.at[mem, :, pl.ds(part * narrow, narrow)],
                send_sem=fwd_send.at[n], recv_sem=fwd_recv.at[n], device_id=target, device_id_type=MESH,
            )
            copy.start()
            forward.append(copy)

    pump(COUNTS[0])

    identity = jnp.where(
        lax.broadcasted_iota(jnp.int32, (members, members), 0)
        == lax.broadcasted_iota(jnp.int32, (members, members), 1),
        1.0, 0.0,
    ).astype(BF16)
    count = count_ref[0]
    bring[chunks].wait()
    bring[chunks + 1].wait()
    for i in range(chunks):
        bring[i].wait()
        here = pl.ds(i * CHUNK, CHUNK)
        position = i * CHUNK + lax.broadcasted_iota(jnp.int32, (1, CHUNK), 1)
        factor = jnp.where(position < count, weight_v[:, here], 0.0)
        flat = lax.dot_general(identity, rows_v[here, :], NT, preferred_element_type=F32)
        scaled_v[:, here] = (flat * factor).astype(BF16)
        misfit = (innov_v[:, here] * factor).astype(BF16)
        misfit_v[:, here] = jnp.broadcast_to(misfit.astype(F32), (16, CHUNK)).astype(BF16)
        pump(COUNTS[1] * (i + 1) // chunks - COUNTS[1] * i // chunks)
    gram = lax.dot_general(scaled_v[...], scaled_v[...], NT, preferred_element_type=F32)
    pull = lax.dot_general(misfit_v[...], scaled_v[...], NT, preferred_element_type=F32)
    row = lax.broadcasted_iota(jnp.int32, (members, members), 0)
    lane = lax.broadcasted_iota(jnp.int32, (members, members), 1)
    pull = pull[:1, :]
    gram = jnp.where((row == 0) & (lane > 0), pull, gram)
    gram = jnp.where((row == 1) & (lane == members - 1), pull[:, :1], gram)
    gram_v[...] = gram.reshape(gram_v.shape)

    sent = []
    def send(source, target, offset):
        n = len(sent)
        copy = pltpu.make_async_remote_copy(
            src_ref=source, dst_ref=target, send_sem=sum_send.at[n], recv_sem=sum_recv.at[n],
            device_id=device(offset), device_id_type=MESH,
        )
        copy.start()
        sent.append(copy)
        return copy

    held, count, levels = gram_v, gram_v.shape[0], len(SCATTER)
    for level, axes in enumerate(SCATTER):
        landing, kept = steps_v[2 * level], steps_v[2 * level + 1]
        part = kept.shape[0]
        arriving = [
            send(held.at[pl.ds(index(axes, offset) * part, part)], landing.at[pl.ds(n * part, part)], offset)
            for n, offset in enumerate(offsets(axes))
        ]
        pump(COUNTS[2 + level])
        total = held[pl.ds(index(axes, {}) * part, part)]
        for n, copy in enumerate(arriving):
            copy.wait_recv()
            total = total + landing[n * part : (n + 1) * part]
        kept[...] = total
        held = kept
    layers_v[z] = held[0]
    arriving = [send(held.at[0], layers_v.at[z], {"z": step}) for step in range(1, Z)]
    pump(COUNTS[4])
    for copy in arriving:
        copy.wait_recv()
    total = layers_v[0]
    for layer in range(1, Z):
        total = total + layers_v[layer]
    held = None
    for level, axes in reversed(list(enumerate(SCATTER))):
        whole = steps_v[2 * levels + level]
        part = steps_v[2 * level + 1].shape[0]
        here = pl.ds(index(axes, {}) * part, part)
        whole[here] = total.reshape((part,) + total.shape[-2:]) if held is None else held[...]
        arriving = [send(whole.at[here], whole.at[here], offset) for offset in offsets(axes)]
        pump(COUNTS[6 - level])
        for copy in arriving:
            copy.wait_recv()
        held = whole
    pump(len(waiting))

    packed = held[...].reshape(members, members)
    pull = jnp.where(lane[:1, :] == 0, packed[1:2, members - 1 :], packed[:1, :])
    picks = jnp.where(lax.broadcasted_iota(jnp.int32, (8, members), 1) == 0, 1.0, 0.0)
    column = lax.dot_general(picks, packed, NT, precision=EXACT, preferred_element_type=F32)[:1, :]
    picks = jnp.where(lax.broadcasted_iota(jnp.int32, (8, members), 1) == 1, 1.0, 0.0)
    second = lax.dot_general(picks, packed, NT, precision=EXACT, preferred_element_type=F32)[:1, :]
    precision = jnp.where(row == 0, column, packed)
    precision = jnp.where((row == 1) & (lane == members - 1), second, precision)
    mat_v[...] = precision + jnp.where(row == lane, members - 1.0, 0.0)
    invert_factor(mat_v, BLOCK, GROUP)
    lower = jnp.where(lane <= row, mat_v[...], 0.0)
    middle = lax.dot_general(pull, lower, NT, precision=EXACT, preferred_element_type=F32)
    shift_w = jnp.dot(middle, lower, precision=EXACT, preferred_element_type=F32)
    mixing = (math.sqrt(members - 1.0) * lower + shift_w).astype(BF16)

    own_in.wait()
    own_out, backward = [], []
    for part in range(SPLIT):
        for copy in forward[part * len(FORDER) : (part + 1) * len(FORDER)]:
            copy.wait_recv()
        for start in range(part * narrow, (part + 1) * narrow, WIDE):
            here = pl.ds(start, WIDE)
            values = block_v[:, :, here].astype(F32).reshape(members, WIDE)
            mean = jnp.sum(values, axis=0, keepdims=True) * (1.0 / members)
            spread = (values - mean).astype(BF16)
            fresh = mean + jnp.dot(mixing, spread, preferred_element_type=F32)
            fresh_v[:, :, here] = fresh.reshape(groups, local, WIDE).astype(BF16)
        here = pl.ds(part * narrow, narrow)
        for offset in ORDER:
            n = len(backward)
            target = member_dev(offset)
            copy = pltpu.make_async_remote_copy(
                src_ref=fresh_v.at[target[0], :, here], dst_ref=out_ref.at[:, cells_of(mem, part)],
                send_sem=bwd_send.at[n], recv_sem=bwd_recv.at[n], device_id=target, device_id_type=MESH,
            )
            copy.start()
            backward.append(copy)
        copy = pltpu.make_async_copy(fresh_v.at[mem, :, here], out_ref.at[:, cells_of(mem, part)], own_sems.at[1 + part])
        copy.start()
        own_out.append(copy)
    for copy in forward:
        copy.wait_send()
    for copy in own_out:
        copy.wait()
    for copy in backward:
        copy.wait()
    for copy in sent:
        copy.wait_send()


def on_device(anomaly, innovation, obs_weight, valid_count, background):
    capacity, members = anomaly.shape
    local, cells = background.shape
    groups = lax.axis_size("mem")
    width = cells // groups
    anywhere = pl.BlockSpec(memory_space=pl.ANY)
    dma = pltpu.SemaphoreType.DMA
    peers = groups - 1
    shards = Y * X * C
    share = members // shards
    scatters, gathers, sends, count = [], [], Z - 1, shards
    for axes in SCATTER:
        size = math.prod(SIZES[axis] for axis in axes)
        part = count // size
        scatters.append(pltpu.VMEM(((size - 1) * part, share, members), F32))
        scatters.append(pltpu.VMEM((part, share, members), F32))
        gathers.append(pltpu.VMEM((count, share, members), F32))
        sends += 2 * (size - 1)
        count = part
    return pl.pallas_call(
        kernel,
        out_shape=pltpu.VMEM(background.shape, background.dtype),
        in_specs=[pl.BlockSpec(memory_space=pltpu.SMEM)] + [anywhere] * 4,
        out_specs=pl.BlockSpec(memory_space=pltpu.VMEM),
        scratch_shapes=[
            pltpu.VMEM((capacity, members), BF16),
            pltpu.VMEM((members, capacity), BF16),
            pltpu.VMEM((16, capacity), BF16),
            pltpu.VMEM((1, capacity), F32),
            pltpu.VMEM((1, capacity), F32),
            pltpu.VMEM((shards, share, members), F32),
            pltpu.VMEM((Z, share, members), F32),
            pltpu.VMEM((members, members), F32),
            pltpu.VMEM((groups, local, width), BF16),
            pltpu.VMEM((groups, local, width), BF16),
            dma((capacity // CHUNK + 2,)),
            dma((SPLIT * peers,)),
            dma((SPLIT * peers,)),
            dma((SPLIT * peers,)),
            dma((SPLIT * peers,)),
            dma((1 + SPLIT,)),
            dma((sends,)),
            dma((sends,)),
            *scatters,
            *gathers,
        ],
        compiler_params=pltpu.CompilerParams(
            collective_id=0, has_side_effects=True, vmem_limit_bytes=56 * 2**20
        ),
        name="analysis",
    )(
        valid_count,
        anomaly,
        innovation.reshape(1, capacity),
        obs_weight.reshape(1, capacity),
        background,
    )


def solution(mesh):
    rows = P(("mem", "cell"))
    slab = P("mem", "cell")
    return jax.shard_map(
        on_device,
        mesh=mesh,
        in_specs=(P(("mem", "cell"), None), rows, rows, rows, slab),
        out_specs=slab,
        check_vma=False,
    )
```

time: 126 us -> 115 us (0.913)
  Pallas kernels: 122 us -> 113 us
  local copies, waits for them, and re-layouts: 3.05 us -> 1.32 us
    pallas_call x1, Pallas kernels: 122 us -> 113 us  [on_device(): pl.pallas_call(kernel, out_shape=pltpu.VMEM(background.shape, background....]
    unnamed x1, local copies, waits for them, and re-layouts: 3.05 us -> 1.32 us
where the time goes in v2:
time: 115 us
  Pallas kernels  113 us (98%)
  local copies, waits for them, and re-layouts  1.32 us (1%)
    pallas_call x1, Pallas kernels, on_device(): pl.pallas_call(kernel, out_shape=pltpu.VMEM(background.shape, background....  113 us

profile of v2, /device:TPU:1, one launch (start us, length us, event | category | flops | bytes accessed | tf_op | source)
XLA Modules:
  0.0 114.8 jit_solution(12093511100802534504)
XLA Ops:
  0.7 112.8 %analysis.1 = bf16[8,131072]{1,0:T(8,128)(2,1)S(1)} custom-call(s32[1]{0:T(128)S(6)} %copy.8.count_ref, bf16[12288,256]{1,0:T(8,128)(2,1)} %anom_ref.1, f32[1,12288]{1,0:T(1,128)} %bitcast.2, f32[1,12288]{1,0:T(1,128)} %bitcast.3, bf16[8,131072]{1,0:T(8,128)(2,1)} %back_ref.1), custom_call_target="tpu_custom_call" | custom-call | tf_op jit(solution)/shard_map/analysis/pallas_call | solution.py:325
  113.5 1.3 %copy.7 = bf16[8,131072]{1,0:T(8,128)(2,1)} copy(bf16[8,131072]{1,0:T(8,128)(2,1)S(1)} %analysis.1) | data formatting | bytes 4194304

commit v3 on v2

--- a/solution.py
+++ b/solution.py
@@ -14,15 +14,27 @@
 NT = (((1,), (1,)), ((), ()))
 
 Z, Y, X, C = 8, 4, 4, 2
-BLOCK, GROUP = 64, 8
+BLOCK = 64
 SPLIT = 2
 CHUNK = 2048
 WIDE = 512
 
 ORDER = [(dz, dy) for dz in (4, 3, 5, 2, 6, 1, 7, 0) for dy in range(Y) if (dz, dy) != (0, 0)]
-FORDER = [(dz, dy) for dys in ((0, 1), (2, 3)) for dz in (1, 7, 2, 6, 0, 4, 3, 5) for dy in dys if (dz, dy) != (0, 0)]
-COUNTS = (12, 12, 8, 2, 2, 2, 8)
+BOTH = [(dz, dy) for dy in (1, 3, 2) for dz in (1, 7, 2, 6, 4, 3, 5)]
+ALONG_Z = [(dz, 0) for dz in (4, 3, 5, 2, 6, 1, 7)]
+ALONG_Y = [(0, dy) for dy in range(1, Y)]
+EARLY = 15
+
+
+def turns(part):
+    return [(part, offset) for offset in BOTH], [(part, offset) for offset in ALONG_Z], [(part, offset) for offset in ALONG_Y]
+
+
+(BOTH_A, Z_A, Y_A), (BOTH_B, Z_B, Y_B) = turns(0), turns(1)
+QUEUE = BOTH_A[:EARLY] + Z_A + BOTH_A[EARLY:] + Y_A + Y_B + Z_B + BOTH_B
+COUNTS = (5, 4, 6, 7, 12, 7, 14, 99)
 SCATTER = (("x", "c"), ("y",))
+GATHER = (("x", "c"), ("y",))
 SIZES = {"z": Z, "y": Y, "x": X, "c": C}
 
 
@@ -41,41 +53,50 @@
     return shifted
 
 
-def small_factor(tile, size, group):
-    lane = lax.broadcasted_iota(jnp.int32, (size, 128), 1)
-    row = lax.broadcasted_iota(jnp.int32, (size, 128), 0)
-    work = jnp.where(lane < size, tile, jnp.where(lane - size == row, 1.0, 0.0))
-
-    def tall(piece):
-        return jnp.concatenate([piece] * (size // 8), axis=0)
-
-    for first in range(0, size, group):
-        spots = range(first, first + group)
-        cols = [jnp.broadcast_to(work[:, j : j + 1], (size, 128)) for j in spots]
-        rows = [jnp.broadcast_to(work[j : j + 1, :], (8, 128)) for j in spots]
-        cross = {
-            (u, v): jnp.broadcast_to(cols[v][first + u : first + u + 1, :], (8, 128))
-            for v in range(group)
-            for u in range(v, group)
-        }
-        for t in range(group):
-            inverse = 1.0 / cross[t, t]
-            for u in range(t + 1, group):
-                ratio = cross[u, t] * inverse
-                rows[u] = rows[u] - ratio * rows[t]
-                cols[u] = cols[u] - tall(ratio) * cols[t]
-                for v in range(u, group):
-                    cross[v, u] = cross[v, u] - ratio * cross[v, t]
-            below = jnp.where(row > first + t, cols[t] * tall(inverse), 0.0)
-            work = work - below * tall(rows[t])
-    diagonal = jnp.sum(jnp.where(lane == row, work, 0.0), axis=1, keepdims=True)
-    scale = lax.rsqrt(diagonal)
-    scale = scale * (1.5 - 0.5 * diagonal * scale * scale)
-    lower = pltpu.roll(work, 128 - size, 1) * scale
-    return jnp.where(lane < size, lower, 0.0)
-
-
-def invert_factor(mat_ref, size, group):
+def small_factor(tile, size):
+    tiles = size // 8
+    lane8 = lax.broadcasted_iota(jnp.int32, (8, 128), 1)
+    row8 = lax.broadcasted_iota(jnp.int32, (8, 128), 0)
+    work = []
+    for g in range(tiles):
+        piece = tile[8 * g : 8 * g + 8, :]
+        work.append(jnp.where(lane8 < size, piece, jnp.where(lane8 - size == row8 + 8 * g, 1.0, 0.0)))
+    for g in range(tiles):
+        first = 8 * g
+        cols = [[jnp.broadcast_to(work[k][:, j : j + 1], (8, 128)) for k in range(g, tiles)] for j in range(first, first + 8)]
+        rows = [jnp.broadcast_to(work[g][j : j + 1, :], (8, 128)) for j in range(8)]
+        cross = {(u, v): jnp.broadcast_to(cols[v][0][u : u + 1, :], (8, 128)) for v in range(8) for u in range(v, 8)}
+        for t in range(0, 8, 2):
+            s = t + 1
+            a, b, c = cross[t, t], cross[s, t], cross[s, s]
+            inv_a = 1.0 / a
+            inv_d = a * (1.0 / (a * c - b * b))
+            f = b * inv_a
+            rows[s] = rows[s] - f * rows[t]
+            cols[s] = [q - f * p for q, p in zip(cols[s], cols[t])]
+            second = {u: cross[u, s] - f * cross[u, t] for u in range(t + 2, 8)}
+            for u in range(t + 2, 8):
+                ru, su = cross[u, t] * inv_a, second[u] * inv_d
+                rows[u] = rows[u] - (ru * rows[t] + su * rows[s])
+                cols[u] = [q - (ru * p + su * r) for q, p, r in zip(cols[u], cols[t], cols[s])]
+                for v in range(u, 8):
+                    cross[v, u] = cross[v, u] - (ru * cross[v, t] + su * second[v])
+            one, two = rows[t] * inv_a, rows[s] * inv_d
+            for k in range(g, tiles):
+                p, r = cols[t][k - g], cols[s][k - g]
+                if k == g:
+                    p, r = jnp.where(row8 > t, p, 0.0), jnp.where(row8 > s, r, 0.0)
+                work[k] = work[k] - (p * one + r * two)
+    lower = []
+    for g in range(tiles):
+        diagonal = jnp.sum(jnp.where(lane8 == row8 + 8 * g, work[g], 0.0), axis=1, keepdims=True)
+        scale = lax.rsqrt(diagonal)
+        scale = scale * (1.5 - 0.5 * diagonal * scale * scale)
+        lower.append(jnp.where(lane8 < size, pltpu.roll(work[g], 128 - size, 1) * scale, 0.0))
+    return jnp.concatenate(lower, axis=0)
+
+
+def invert_factor(mat_ref, size):
     order = mat_ref.shape[0]
     for first in range(0, order, size):
         last = first + size
@@ -85,7 +106,7 @@
         tile = rows[:, base : base + 128]
         if shift:
             tile = pltpu.roll(tile, 128 - shift, 1)
-        inverse = small_factor(tile, size, group)
+        inverse = small_factor(tile, size)
         panel = jnp.dot(inverse[:, :size], rows, precision=EXACT, preferred_element_type=F32)
         placed = pltpu.roll(inverse, shift, 1) if shift else inverse
         blank = jnp.zeros_like(placed)
@@ -104,7 +125,7 @@
 def kernel(
     count_ref, anom_ref, innov_ref, weight_ref, back_ref, out_ref,
     rows_v, scaled_v, misfit_v, innov_v, weight_v, gram_v, layers_v, mat_v, block_v, fresh_v,
-    in_sems, fwd_send, fwd_recv, bwd_send, bwd_recv, own_sems, sum_send, sum_recv, *steps_v,
+    count_v, in_sems, fwd_send, fwd_recv, bwd_send, bwd_recv, own_sems, sum_send, sum_recv, *steps_v,
 ):
     mem, cell = lax.axis_index("mem"), lax.axis_index("cell")
     place = {
@@ -139,16 +160,17 @@
     ]
     bring.append(pltpu.make_async_copy(innov_ref, innov_v, in_sems.at[chunks]))
     bring.append(pltpu.make_async_copy(weight_ref, weight_v, in_sems.at[chunks + 1]))
-    for copy in bring:
+    bring.append(pltpu.make_async_copy(count_ref, count_v, in_sems.at[chunks + 2]))
+    for copy in bring[chunks:] + bring[:chunks]:
         copy.start()
 
     barrier = pltpu.get_barrier_semaphore()
     greeted = [{"z": dz, "y": dy} for dz, dy in ORDER]
-    for axes in SCATTER:
+    for axes in SCATTER + GATHER:
         for offset in offsets(axes):
-            if not set(axes) <= {"z", "y"}:
-                if any(offset.get(axis, 0) for axis in "xc"):
-                    greeted.append(offset)
+            offset = {axis: step for axis, step in offset.items() if step}
+            if offset not in greeted and ("x" in offset or "c" in offset):
+                greeted.append(offset)
     for offset in greeted:
         pl.semaphore_signal(barrier, inc=1, device_id=device(offset), device_id_type=MESH)
     pl.semaphore_wait(barrier, len(greeted))
@@ -162,11 +184,10 @@
         back_ref.at[:, pl.ds(pl.multiple_of(mem * width, width), width)], block_v.at[mem], own_sems.at[0]
     )
     own_in.start()
-    waiting = [(part, offset) for part in range(SPLIT) for offset in FORDER]
     forward = []
 
     def pump(count):
-        for part, offset in waiting[len(forward) : len(forward) + count]:
+        for part, offset in QUEUE[len(forward) : len(forward) + count]:
             n = len(forward)
             target = member_dev(offset)
             copy = pltpu.make_async_remote_copy(
@@ -175,7 +196,7 @@
                 send_sem=fwd_send.at[n], recv_sem=fwd_recv.at[n], device_id=target, device_id_type=MESH,
             )
             copy.start()
-            forward.append(copy)
+            forward.append((part, copy))
 
     pump(COUNTS[0])
 
@@ -184,9 +205,9 @@
         == lax.broadcasted_iota(jnp.int32, (members, members), 1),
         1.0, 0.0,
     ).astype(BF16)
-    count = count_ref[0]
-    bring[chunks].wait()
-    bring[chunks + 1].wait()
+    for copy in bring[chunks:]:
+        copy.wait()
+    count = count_v[0]
     for i in range(chunks):
         bring[i].wait()
         here = pl.ds(i * CHUNK, CHUNK)
@@ -240,18 +261,18 @@
     total = layers_v[0]
     for layer in range(1, Z):
         total = total + layers_v[layer]
-    held = None
-    for level, axes in reversed(list(enumerate(SCATTER))):
+    held = total.reshape((1,) + total.shape)
+    for level, axes in reversed(list(enumerate(GATHER))):
         whole = steps_v[2 * levels + level]
-        part = steps_v[2 * level + 1].shape[0]
+        part = held.shape[0]
         here = pl.ds(index(axes, {}) * part, part)
-        whole[here] = total.reshape((part,) + total.shape[-2:]) if held is None else held[...]
+        whole[here] = held[...]
         arriving = [send(whole.at[here], whole.at[here], offset) for offset in offsets(axes)]
         pump(COUNTS[6 - level])
         for copy in arriving:
             copy.wait_recv()
         held = whole
-    pump(len(waiting))
+    pump(COUNTS[7])
 
     packed = held[...].reshape(members, members)
     pull = jnp.where(lane[:1, :] == 0, packed[1:2, members - 1 :], packed[:1, :])
@@ -262,7 +283,7 @@
     precision = jnp.where(row == 0, column, packed)
     precision = jnp.where((row == 1) & (lane == members - 1), second, precision)
     mat_v[...] = precision + jnp.where(row == lane, members - 1.0, 0.0)
-    invert_factor(mat_v, BLOCK, GROUP)
+    invert_factor(mat_v, BLOCK)
     lower = jnp.where(lane <= row, mat_v[...], 0.0)
     middle = lax.dot_general(pull, lower, NT, precision=EXACT, preferred_element_type=F32)
     shift_w = jnp.dot(middle, lower, precision=EXACT, preferred_element_type=F32)
@@ -271,8 +292,9 @@
     own_in.wait()
     own_out, backward = [], []
     for part in range(SPLIT):
-        for copy in forward[part * len(FORDER) : (part + 1) * len(FORDER)]:
-            copy.wait_recv()
+        for owner, copy in forward:
+            if owner == part:
+                copy.wait_recv()
         for start in range(part * narrow, (part + 1) * narrow, WIDE):
             here = pl.ds(start, WIDE)
             values = block_v[:, :, here].astype(F32).reshape(members, WIDE)
@@ -293,7 +315,7 @@
         copy = pltpu.make_async_copy(fresh_v.at[mem, :, here], out_ref.at[:, cells_of(mem, part)], own_sems.at[1 + part])
         copy.start()
         own_out.append(copy)
-    for copy in forward:
+    for _, copy in forward:
         copy.wait_send()
     for copy in own_out:
         copy.wait()
@@ -319,13 +341,18 @@
         part = count // size
         scatters.append(pltpu.VMEM(((size - 1) * part, share, members), F32))
         scatters.append(pltpu.VMEM((part, share, members), F32))
+        sends += size - 1
+        count = part
+    count = shards
+    for axes in GATHER:
+        size = math.prod(SIZES[axis] for axis in axes)
         gathers.append(pltpu.VMEM((count, share, members), F32))
-        sends += 2 * (size - 1)
-        count = part
+        sends += size - 1
+        count //= size
     return pl.pallas_call(
         kernel,
         out_shape=pltpu.VMEM(background.shape, background.dtype),
-        in_specs=[pl.BlockSpec(memory_space=pltpu.SMEM)] + [anywhere] * 4,
+        in_specs=[anywhere] * 5,
         out_specs=pl.BlockSpec(memory_space=pltpu.VMEM),
         scratch_shapes=[
             pltpu.VMEM((capacity, members), BF16),
@@ -338,7 +365,8 @@
             pltpu.VMEM((members, members), F32),
             pltpu.VMEM((groups, local, width), BF16),
             pltpu.VMEM((groups, local, width), BF16),
-            dma((capacity // CHUNK + 2,)),
+            pltpu.SMEM((1,), jnp.int32),
+            dma((capacity // CHUNK + 3,)),
             dma((SPLIT * peers,)),
             dma((SPLIT * peers,)),
             dma((SPLIT * peers,)),

time: 115 us -> 111 us (0.965)
  Pallas kernels: 113 us -> 109 us
    pallas_call x1, Pallas kernels: 113 us -> 109 us  [on_device(): pl.pallas_call(kernel, out_shape=pltpu.VMEM(background.shape, background....]
where the time goes in v3:
time: 111 us
  Pallas kernels  109 us (98%)
  local copies, waits for them, and re-layouts  1.32 us (1%)
    pallas_call x1, Pallas kernels, on_device(): pl.pallas_call(kernel, out_shape=pltpu.VMEM(background.shape, background....  109 us

profile of v3, /device:TPU:1, one launch (start us, length us, event | category | flops | bytes accessed | tf_op | source)
XLA Modules:
  0.0 110.8 jit_solution(18362243006081338113)
XLA Ops:
  0.7 108.8 %analysis.1 = bf16[8,131072]{1,0:T(8,128)(2,1)S(1)} custom-call(s32[1]{0:T(128)S(6)} %copy.8.count_ref, bf16[12288,256]{1,0:T(8,128)(2,1)} %anom_ref.1, f32[1,12288]{1,0:T(1,128)} %bitcast.2, f32[1,12288]{1,0:T(1,128)} %bitcast.3, bf16[8,131072]{1,0:T(8,128)(2,1)} %back_ref.1), custom_call_target="tpu_custom_call" | custom-call | tf_op jit(solution)/shard_map/analysis/pallas_call | solution.py:352
  109.4 1.3 %copy.7 = bf16[8,131072]{1,0:T(8,128)(2,1)} copy(bf16[8,131072]{1,0:T(8,128)(2,1)S(1)} %analysis.1) | data formatting | bytes 4194304

commit v4 on v3

--- a/solution.py
+++ b/solution.py
@@ -19,7 +19,7 @@
 CHUNK = 2048
 WIDE = 512
 
-ORDER = [(dz, dy) for dz in (4, 3, 5, 2, 6, 1, 7, 0) for dy in range(Y) if (dz, dy) != (0, 0)]
+ORDER = [(dz, dy) for dz in (0, 4, 3, 5, 2, 6, 1, 7) for dy in (2, 1, 3, 0) if (dz, dy) != (0, 0)]
 BOTH = [(dz, dy) for dy in (1, 3, 2) for dz in (1, 7, 2, 6, 4, 3, 5)]
 ALONG_Z = [(dz, 0) for dz in (4, 3, 5, 2, 6, 1, 7)]
 ALONG_Y = [(0, dy) for dy in range(1, Y)]
@@ -161,8 +161,6 @@
     bring.append(pltpu.make_async_copy(innov_ref, innov_v, in_sems.at[chunks]))
     bring.append(pltpu.make_async_copy(weight_ref, weight_v, in_sems.at[chunks + 1]))
     bring.append(pltpu.make_async_copy(count_ref, count_v, in_sems.at[chunks + 2]))
-    for copy in bring[chunks:] + bring[:chunks]:
-        copy.start()
 
     barrier = pltpu.get_barrier_semaphore()
     greeted = [{"z": dz, "y": dy} for dz, dy in ORDER]
@@ -173,6 +171,8 @@
                 greeted.append(offset)
     for offset in greeted:
         pl.semaphore_signal(barrier, inc=1, device_id=device(offset), device_id_type=MESH)
+    for copy in bring[chunks:] + bring[:chunks]:
+        copy.start()
     pl.semaphore_wait(barrier, len(greeted))
 
     narrow = width // SPLIT
@@ -276,12 +276,10 @@
 
     packed = held[...].reshape(members, members)
     pull = jnp.where(lane[:1, :] == 0, packed[1:2, members - 1 :], packed[:1, :])
-    picks = jnp.where(lax.broadcasted_iota(jnp.int32, (8, members), 1) == 0, 1.0, 0.0)
-    column = lax.dot_general(picks, packed, NT, precision=EXACT, preferred_element_type=F32)[:1, :]
-    picks = jnp.where(lax.broadcasted_iota(jnp.int32, (8, members), 1) == 1, 1.0, 0.0)
-    second = lax.dot_general(picks, packed, NT, precision=EXACT, preferred_element_type=F32)[:1, :]
-    precision = jnp.where(row == 0, column, packed)
-    precision = jnp.where((row == 1) & (lane == members - 1), second, precision)
+    picks = jnp.where(row[:8, :] == lane[:8, :], 1.0, 0.0)
+    columns = lax.dot_general(picks, packed, NT, precision=EXACT, preferred_element_type=F32)
+    precision = jnp.where(row == 0, columns[:1, :], packed)
+    precision = jnp.where((row == 1) & (lane == members - 1), columns[1:2, :], precision)
     mat_v[...] = precision + jnp.where(row == lane, members - 1.0, 0.0)
     invert_factor(mat_v, BLOCK)
     lower = jnp.where(lane <= row, mat_v[...], 0.0)
@@ -315,14 +313,14 @@
         copy = pltpu.make_async_copy(fresh_v.at[mem, :, here], out_ref.at[:, cells_of(mem, part)], own_sems.at[1 + part])
         copy.start()
         own_out.append(copy)
-    for _, copy in forward:
+    for copy in [copy for _, copy in forward] + sent:
         copy.wait_send()
     for copy in own_out:
         copy.wait()
     for copy in backward:
-        copy.wait()
-    for copy in sent:
         copy.wait_send()
+    for copy in backward:
+        copy.wait_recv()
 
 
 def on_device(anomaly, innovation, obs_weight, valid_count, background):

time: 111 us -> 110 us (level)
  no operation moved by 1% of the time
where the time goes in v4:
time: 110 us
  Pallas kernels  108 us (98%)
  local copies, waits for them, and re-layouts  1.32 us (1%)
    pallas_call x1, Pallas kernels, on_device(): pl.pallas_call(kernel, out_shape=pltpu.VMEM(background.shape, background....  108 us

profile of v4, /device:TPU:1, one launch (start us, length us, event | category | flops | bytes accessed | tf_op | source)
XLA Modules:
  0.0 110.3 jit_solution(16772625474130956961)
XLA Ops:
  0.7 108.3 %analysis.1 = bf16[8,131072]{1,0:T(8,128)(2,1)S(1)} custom-call(s32[1]{0:T(128)S(6)} %copy.8.count_ref, bf16[12288,256]{1,0:T(8,128)(2,1)} %anom_ref.1, f32[1,12288]{1,0:T(1,128)} %bitcast.2, f32[1,12288]{1,0:T(1,128)} %bitcast.3, bf16[8,131072]{1,0:T(8,128)(2,1)} %back_ref.1), custom_call_target="tpu_custom_call" | custom-call | tf_op jit(solution)/shard_map/analysis/pallas_call | solution.py:350
  108.9 1.3 %copy.7 = bf16[8,131072]{1,0:T(8,128)(2,1)} copy(bf16[8,131072]{1,0:T(8,128)(2,1)S(1)} %analysis.1) | data formatting | bytes 4194304
